TPU v7x, 256 devices: a whole 4x4x8 slice. The times are simulated.
256 devices in a mesh: row: 16 (over z, core), col: 16 (over x, y).
Axes of the slice: x: 4, y: 4, z: 8, core: 2. Of those that a mesh axis runs over, the one named last changes fastest.
Arguments:
- tiles: bfloat16 [16, 16, 64, 256, 256], P('row', 'col'), may hold values from -0.21875 to 0.21875
- tile_row: int32 [16, 16, 64], P('row', 'col'), may hold values from 0 to 63
- tile_col: int32 [16, 16, 64], P('row', 'col'), may hold values from 0 to 255
- live_count: int32 [16, 16], P('row', 'col'), may hold values from 16 to 64, as said below
- cost: float32 [1048576], P('col'), may hold values from -6 to 6
- upper: float32 [1048576], P('col'), may hold values from 0.5 to 2
- capacity: float32 [262144], P('row'), may hold values from 0.05 to 0.5
- step_sizes: float32 [2], replicated, may hold values from 0.2 to 0.6
- restart_flags: int32 [4], replicated, may hold values from 0 to 1
Outputs:
- primal: float32 [1048576], P('col')
- dual: float32 [262144], P('row')
- movement: float32 [4], replicated
Inputs may be any that keep to these rules, and one draw needn't show every extreme that they name: `live_count`: at least one device uses all 64 slots.
All inputs are finite; a program needn't handle non-finite values.
Results may differ from a plain program's by a relative error of at most 0.0075.
Values sent between devices are 32-bit elements; how exact they have to be, the bound alone decides.
A program may use at most 64 MiB of HBM per device.

v0:
```python
import jax
import jax.numpy as jnp
from jax import lax
from jax.sharding import PartitionSpec as P

ITERS = 4


def shards(tiles, tile_row, tile_col, live_count, cost, upper, capacity, step_sizes, restart_flags):
    tile_set = tiles[0, 0]
    rows_idx = tile_row[0, 0]
    cols_idx = tile_col[0, 0]
    count = live_count[0, 0]
    slots = tile_set.shape[0]
    width = tile_set.shape[1]
    col_blocks = cost.shape[0] // width
    row_blocks = capacity.shape[0] // width
    live = (lax.iota(jnp.int32, slots) < count).astype(jnp.float32)
    col_table = (cols_idx[:, None] == lax.iota(jnp.int32, col_blocks)[None, :]).astype(
        jnp.float32
    ) * live[:, None]
    row_table = (rows_idx[:, None] == lax.iota(jnp.int32, row_blocks)[None, :]).astype(
        jnp.float32
    ) * live[:, None]
    tau = step_sizes[0]
    sigma = step_sizes[1]

    def transpose_terms(dual_low):
        picked = dual_low.reshape(row_blocks, width)[rows_idx]
        terms = jnp.einsum("tij,ti->tj", tile_set, picked, preferred_element_type=jnp.float32)
        return jnp.dot(col_table.T, terms, precision=lax.Precision.HIGHEST).reshape(-1)

    def forward_terms(extended):
        picked = extended.reshape(col_blocks, width)[cols_idx]
        terms = jnp.einsum("tij,tj->ti", tile_set, picked, preferred_element_type=jnp.float32)
        return jnp.dot(row_table.T, terms, precision=lax.Precision.HIGHEST).reshape(-1)

    primal = jnp.zeros_like(cost)
    dual = jnp.zeros_like(capacity)
    sum_primal = jnp.zeros_like(cost)
    sum_dual = jnp.zeros_like(capacity)
    counter = jnp.zeros((), jnp.float32)
    moves = []
    for step in range(ITERS):
        gradient_part = transpose_terms(dual.astype(jnp.bfloat16))
        gradient = lax.psum(gradient_part, "row")
        primal_new = jnp.clip(primal - tau * (cost + gradient), 0.0, upper)
        extended = (2.0 * primal_new - primal).astype(jnp.bfloat16)
        load_part = forward_terms(extended)
        load = lax.psum(load_part, "col")
        dual_new = jnp.maximum(dual + sigma * (load - capacity), 0.0)
        primal_step = primal_new - primal
        dual_step = dual_new - dual
        primal_square = lax.psum(jnp.sum(primal_step * primal_step), "col")
        dual_square = lax.psum(jnp.sum(dual_step * dual_step), "row")
        moves.append(jnp.sqrt(primal_square / tau + dual_square / sigma + 1e-06))
        sum_primal = sum_primal + primal_new
        sum_dual = sum_dual + dual_new
        counter = counter + 1.0
        flag = restart_flags[step] == 1
        primal = jnp.where(flag, sum_primal / counter, primal_new)
        dual = jnp.where(flag, sum_dual / counter, dual_new)
        sum_primal = jnp.where(flag, 0.0, sum_primal)
        sum_dual = jnp.where(flag, 0.0, sum_dual)
        counter = jnp.where(flag, 0.0, counter)
    return (primal, dual, jnp.stack(moves))


def solution(mesh):
    in_specs = (
        P("row", "col", None, None, None),
        P("row", "col", None),
        P("row", "col", None),
        P("row", "col"),
        P("col"),
        P("col"),
        P("row"),
        P(),
        P(),
    )
    out_specs = (P("col"), P("row"), P())
    return jax.shard_map(shards, mesh=mesh, in_specs=in_specs, out_specs=out_specs, check_vma=False)
```

profile of v0, /device:TPU:1, one launch (start us, length us, event | category | flops | bytes accessed | tf_op | source)
XLA Modules:
  0.0 922.0 jit_solution(2701341757938687059)
XLA Ops:
  9.3 4.6 fusion.14
  14.4 0.8 copy.28
  16.0 111.6 %all-reduce.11.cloned.1.call-done = f32[65536]{0:T(1024)} async-done(((f32[65536]{0:T(1024)}), f32[65536]{0:T(1024)}) %all-reduce.11.cloned.1.call-update) | async-done | bytes 262160 | tf_op jit(solution)/shard_map/psum | solution.py:46
  127.6 1.6 multiply_convert_fusion
  130.0 5.6 fusion.12
  136.7 89.9 %all-reduce.13.cloned.1.call-done = f32[16384]{0:T(1024)} async-done(((f32[16384]{0:T(1024)}), f32[16384]{0:T(1024)}) %all-reduce.13.cloned.1.call-update) | async-done | bytes 65552 | tf_op jit(solution)/shard_map/psum | solution.py:50
  226.6 1.5 fusion.83
  228.1 0.7 gather_fusion.2
  228.8 4.6 fusion.10
  233.9 0.8 copy.30
  234.8 109.6 %all-reduce.15.cloned.1.call-done = f32[65536]{0:T(1024)} async-done(((f32[65536]{0:T(1024)}), f32[65536]{0:T(1024)}) %all-reduce.15.cloned.1.call-update) | async-done | bytes 262160 | tf_op jit(solution)/shard_map/psum | solution.py:46
  344.4 2.3 multiply_reduce_fusion.3
  347.5 5.6 fusion.8
  356.1 88.1 %all-reduce.17.cloned.1.call-done = f32[16384]{0:T(1024)} async-done(((f32[16384]{0:T(1024)}), f32[16384]{0:T(1024)}) %all-reduce.17.cloned.1.call-update) | async-done | bytes 65552 | tf_op jit(solution)/shard_map/psum | solution.py:50
  444.2 1.5 fusion.84
  446.4 4.6 fusion.6
  451.5 0.8 copy.32
  452.4 109.6 %all-reduce.19.cloned.1.call-done = f32[65536]{0:T(1024)} async-done(((f32[65536]{0:T(1024)}), f32[65536]{0:T(1024)}) %all-reduce.19.cloned.1.call-update) | async-done | bytes 262160 | tf_op jit(solution)/shard_map/psum | solution.py:46
  562.0 2.3 multiply_reduce_fusion.1
  565.0 5.6 fusion.4
  572.4 89.3 %all-reduce.21.cloned.1.call-done = f32[16384]{0:T(1024)} async-done(((f32[16384]{0:T(1024)}), f32[16384]{0:T(1024)}) %all-reduce.21.cloned.1.call-update) | async-done | bytes 65552 | tf_op jit(solution)/shard_map/psum | solution.py:50
  661.7 1.5 fusion.60
  663.9 4.6 fusion.2
  669.0 0.8 copy.34
  670.6 108.9 %all-reduce.23.cloned.1.call-done = f32[65536]{0:T(1024)} async-done(((f32[65536]{0:T(1024)}), f32[65536]{0:T(1024)}) %all-reduce.23.cloned.1.call-update) | async-done | bytes 262160 | tf_op jit(solution)/shard_map/psum | solution.py:46
  779.5 2.3 multiply_reduce_fusion
  781.8 0.8 subtract_convert_fusion
  783.4 5.6 fusion
  790.0 33.8 %all-reduce = (f32[]{:T(128)}, f32[]{:T(128)}, f32[]{:T(128)}, f32[]{:T(128)}) all-reduce(f32[]{:T(128)} %get-tuple-element.21, f32[]{:T(128)} %get-tuple-element.18, f32[]{:T(128)} %get-tuple-element.4, f32[]{:T(128)} %get-tuple-element.3), channel_id=1, replica_groups=mesh['row'=16,'col'=16] {'col'}, use_global_device_ids=true, to_apply=%region_21.22 | all-reduce | flops 4 | bytes 32 | tf_op jit(solution)/shard_map/psum | solution.py:54
  829.0 51.1 %all-reduce.25.cloned.1.call-done = f32[16384]{0:T(1024)} async-done(((f32[16384]{0:T(1024)}), f32[16384]{0:T(1024)}) %all-reduce.25.cloned.1.call-update) | async-done | bytes 65552 | tf_op jit(solution)/shard_map/psum | solution.py:50
  880.1 2.8 multiply_reduce_fusion.6
  882.9 26.3 %all-reduce.1 = (f32[]{:T(128)}, f32[]{:T(128)}, f32[]{:T(128)}, f32[]{:T(128)}) all-reduce(f32[]{:T(128)} %get-tuple-element.6, f32[]{:T(128)} %get-tuple-element.8, f32[]{:T(128)} %get-tuple-element.5, f32[]{:T(128)} %get-tuple-element.7), channel_id=1, replica_groups=mesh['row'=16,'col'=16] {'row'}, use_global_device_ids=true, to_apply=%region_23.24 | all-reduce | flops 4 | bytes 32 | tf_op jit(solution)/shard_map/psum | solution.py:55
  (71 shorter events, 14.2 us)
Async XLA Ops:
  7.2 6.8 copy-start.5
  7.2 120.4 %all-reduce.11.cloned.1.call-start = ((), (), s32[]{:S(2)}) async-start(), calls=%async_computation | async-start | bytes 524288 | tf_op jit(solution)/shard_map/psum | solution.py:46
  9.3 6.1 copy-start.8
  9.3 118.3 %copy-start = (f32[65536]{0:T(1024)S(1)}, f32[65536]{0:T(1024)}, u32[]{:S(2)}) copy-start(f32[65536]{0:T(1024)} %param.14) | copy-start | bytes 786436
  9.3 118.3 %copy-start.1 = (f32[65536]{0:T(1024)S(1)}, f32[65536]{0:T(1024)}, u32[]{:S(2)}) copy-start(f32[65536]{0:T(1024)} %param.13) | copy-start | bytes 786436
  13.9 121.7 %copy-start.6 = (s32[1,1,64]{2,1,0:T(1,128)S(1)}, s32[1,1,64]{2,1,0:T(1,128)}, u32[]{:S(2)}) copy-start(s32[1,1,64]{2,1,0:T(1,128)} %param.10) | copy-start | bytes 772
  13.9 212.7 %copy-start.2 = (f32[16384]{0:T(1024)S(1)}, f32[16384]{0:T(1024)}, u32[]{:S(2)}) copy-start(f32[16384]{0:T(1024)} %param.15) | copy-start | bytes 196612
  15.3 211.3 %all-reduce.13.cloned.1.call-start = ((), (), s32[]{:S(2)}) async-start(), calls=%async_computation.1 | async-start | bytes 131072 | tf_op jit(solution)/shard_map/psum | solution.py:50
  136.7 207.7 %all-reduce.15.cloned.1.call-start = ((), (), s32[]{:S(2)}) async-start(), calls=%async_computation.2 | async-start | bytes 524288 | tf_op jit(solution)/shard_map/psum | solution.py:46
  233.4 120.9 %copy-start.7 = (s32[4]{0:T(128)S(1)}, s32[4]{0:T(128)}, u32[]{:S(2)}) copy-start(s32[4]{0:T(128)} %param.17) | copy-start | bytes 52
  233.4 210.8 %copy-start.3 = (f32[16384]{0:T(1024)S(1)}, f32[16384]{0:T(1024)}, u32[]{:S(2)}) copy-start(f32[16384]{0:T(1024)} %all-reduce.13.cloned.1.call-done) | copy-start | bytes 196612
  234.8 209.4 %all-reduce.17.cloned.1.call-start = ((), (), s32[]{:S(2)}) async-start(), calls=%async_computation.3 | async-start | bytes 131072 | tf_op jit(solution)/shard_map/psum | solution.py:50
  354.2 207.8 %all-reduce.19.cloned.1.call-start = ((), (), s32[]{:S(2)}) async-start(), calls=%async_computation.4 | async-start | bytes 524288 | tf_op jit(solution)/shard_map/psum | solution.py:46
  451.0 210.7 %copy-start.4 = (f32[16384]{0:T(1024)S(1)}, f32[16384]{0:T(1024)}, u32[]{:S(2)}) copy-start(f32[16384]{0:T(1024)} %all-reduce.17.cloned.1.call-done) | copy-start | bytes 196612
  452.3 209.4 %all-reduce.21.cloned.1.call-start = ((), (), s32[]{:S(2)}) async-start(), calls=%async_computation.5 | async-start | bytes 131072 | tf_op jit(solution)/shard_map/psum | solution.py:50
  571.7 207.8 %all-reduce.23.cloned.1.call-start = ((), (), s32[]{:S(2)}) async-start(), calls=%async_computation.6 | async-start | bytes 524288 | tf_op jit(solution)/shard_map/psum | solution.py:46
  669.9 210.2 %all-reduce.25.cloned.1.call-start = ((), (), s32[]{:S(2)}) async-start(), calls=%async_computation.7 | async-start | bytes 131072 | tf_op jit(solution)/shard_map/psum | solution.py:50
Sparse Core Ops, SparseCore 0:
  15.4 112.1 all-reduce.10
  136.8 89.7 all-reduce.12
  234.9 109.4 all-reduce.14
  354.3 89.7 all-reduce.16
  452.4 109.4 all-reduce.18
  571.8 89.8 all-reduce.20
  670.0 109.4 all-reduce.22
  790.1 89.8 all-reduce.24
where the time goes:
time: 923 us; the launch traced here: 922 us
  waiting for transfers between devices  758 us (82%)
  blocking collectives  60.1 us (7%)
  matrix products  44.2 us (5%)
  between operations  28.1 us (3%)
  other arithmetic  18 us (2%)
  local copies, waits for them, and re-layouts  13.2 us (1%)
    psum x4, waiting for transfers between devices, shards(): gradient = lax.psum(gradient_part, 'row')  440 us
    psum x4, waiting for transfers between devices, shards(): load = lax.psum(load_part, 'col')  318 us
    psum x1, blocking collectives, shards(): primal_square = lax.psum(jnp.sum(primal_step * primal_step), 'col')  33.8 us
    psum x1, blocking collectives, shards(): dual_square = lax.psum(jnp.sum(dual_step * dual_step), 'row')  26.3 us
    dot_general x4, matrix products, forward_terms(): jnp.einsum('tij,tj->ti', tile_set, picked, preferred_element_type=jnp.flo...  22.5 us
  transfers between devices with their start and end apart: 8, of which 8 were waited for; matrix products, arithmetic and copies ran while one was open for 0% of the time, Pallas kernels for 0%

commit v1 on v0

v1 whole, which is shorter than its diff:
```python
import functools

import jax
import jax.numpy as jnp
from jax import lax
from jax.experimental import pallas as pl
from jax.experimental.pallas import tpu as pltpu
from jax.sharding import PartitionSpec as P

ITERS = 4
LANES = 128
GROUP = 16
MESH = pl.DeviceIdType.MESH


def split_dot(table, values):
    high = values.astype(jnp.bfloat16)
    rest = values - high.astype(jnp.float32)
    mid = rest.astype(jnp.bfloat16)
    low = (rest - mid.astype(jnp.float32)).astype(jnp.bfloat16)
    out = jnp.dot(table, low, preferred_element_type=jnp.float32)
    out += jnp.dot(table, mid, preferred_element_type=jnp.float32)
    return out + jnp.dot(table, high, preferred_element_type=jnp.float32)


def kernel(
    n_row, n_col,
    tiles_hbm, col_ref, row_ref, cost_hbm, upper_hbm, cap_hbm, count_ref, step_ref, flag_ref,
    primal_out, dual_out, move_out,
    tiles, cost, upper, cap, col_table, col_pick, row_table, row_pick,
    primal, sum_primal, dual, sum_dual, picked, terms,
    grad, pair_in, pair_sum, ring_in, primal_new, load, load_in, dual_new,
    primal_sq, dual_sq, primal_sq_in, dual_sq_in,
    tile_sem, in_sem, out_sem,
    pair_send, pair_recv, ring_send, ring_recv, gather_send, gather_recv, half_send, half_recv,
    load_send, load_recv, dual_send, dual_recv, sq_send, sq_recv,
):
    r = lax.axis_index("row")
    c = lax.axis_index("col")
    z, core = lax.div(r, 2), lax.rem(r, 2)
    n_z = n_row // 2
    slots, width = tiles.shape[0], tiles.shape[1]
    p_rows, d_rows = primal.shape[0], dual.shape[0]
    p_half, p_share, d_share = p_rows // 2, p_rows // n_row, d_rows // n_col
    groups = slots // GROUP
    sibling = (2 * z + 1 - core, c)

    def tile_copy(g):
        part = pl.ds(g * GROUP, GROUP)
        return pltpu.make_async_copy(tiles_hbm.at[part], tiles.at[part], tile_sem.at[g])

    for g in range(groups):
        tile_copy(g).start()
    in_copies = [
        pltpu.make_async_copy(src, dst, in_sem.at[i])
        for i, (src, dst) in enumerate(((cost_hbm, cost), (upper_hbm, upper), (cap_hbm, cap)))
    ]
    for copy in in_copies:
        copy.start()

    barrier = pltpu.get_barrier_semaphore()
    for o in range(1, n_row):
        pl.semaphore_signal(barrier, inc=1, device_id=(lax.rem(r + o, n_row), c), device_id_type=MESH)
    for o in range(1, n_col):
        pl.semaphore_signal(barrier, inc=1, device_id=(r, lax.rem(c + o, n_col)), device_id_type=MESH)

    lane = lax.broadcasted_iota(jnp.int32, (1, 2 * slots), 1)
    live = lax.rem(lane, slots) < count_ref[0, 0]

    def tables(index_ref, n_rows, table, pick):
        twice = index_ref[...] * 2
        key = jnp.where(live, jnp.concatenate([twice, twice + 1], axis=1), -1)
        hot = jnp.where(lax.broadcasted_iota(jnp.int32, (n_rows, 2 * slots), 0) == key, 1.0, 0.0)
        table[...] = hot.astype(jnp.bfloat16)
        pick[...] = hot.T.astype(jnp.bfloat16)

    tables(col_ref, p_rows, col_table, col_pick)
    tables(row_ref, d_rows, row_table, row_pick)
    for ref in (primal, sum_primal, dual, sum_dual, primal_sq, dual_sq):
        ref[...] = jnp.zeros_like(ref)
    tau, sigma = step_ref[0], step_ref[1]
    for copy in in_copies:
        copy.wait()
    for g in range(groups):
        tile_copy(g).wait()
    pl.semaphore_wait(barrier, n_row - 1 + n_col - 1)

    def pick_blocks(pick, values):
        both = jnp.dot(pick[...], values.astype(jnp.bfloat16), preferred_element_type=jnp.float32)
        picked[...] = jnp.concatenate([both[:slots], both[slots:]], axis=1).astype(jnp.bfloat16)

    def place_terms(table):
        both = jnp.concatenate([terms[:, :LANES], terms[:, LANES:]], axis=0)
        return split_dot(table[...], both)

    def transposed_product():
        at_row = lax.broadcasted_iota(jnp.int32, (GROUP, GROUP * width), 0)
        at_tile = lax.div(lax.broadcasted_iota(jnp.int32, (GROUP, GROUP * width), 1), width)
        for g in range(groups):
            part = pl.ds(g * GROUP, GROUP)
            wide = jnp.concatenate([picked[part, :]] * GROUP, axis=1)
            left = jnp.where(at_row == at_tile, wide, jnp.zeros((), jnp.bfloat16))
            right = tiles[part].reshape(GROUP * width, width)
            terms[part, :] = jnp.dot(left, right, preferred_element_type=jnp.float32)

    def forward_product():
        at_row = lax.broadcasted_iota(jnp.int32, (GROUP, width), 0)

        def group(g, _):
            part = pl.ds(pl.multiple_of(g * GROUP, GROUP), GROUP)
            mine = picked[part, :]
            total = jnp.zeros((GROUP, width), jnp.float32)
            for s in range(GROUP):
                left = jnp.where(at_row == s, mine, jnp.zeros((), jnp.bfloat16))
                total += lax.dot_general(
                    left, tiles[g * GROUP + s], (((1,), (1,)), ((), ())), preferred_element_type=jnp.float32
                )
            terms[part, :] = total
            return 0

        lax.fori_loop(0, groups, group, 0)

    def p_part(which_core, which_z):
        return pl.ds(pl.multiple_of(which_core * p_half + which_z * p_share, 8), p_share)

    def half_part(which_z):
        return pl.ds(pl.multiple_of(which_z * p_share, 8), p_share)

    def d_part(which):
        return pl.ds(pl.multiple_of(which * d_share, 8), d_share)

    def remote(src, dst, send, recv, device):
        return pltpu.make_async_remote_copy(
            src_ref=src, dst_ref=dst, send_sem=send, recv_sem=recv, device_id=device, device_id_type=MESH
        )

    far_first = sorted(range(1, n_z), key=lambda o: -min(o, n_z - o))
    own_p = p_part(core, z)
    own_d = d_part(c)
    other_core = 1 - core

    def iteration(k, counter):
        pick_blocks(row_pick, dual[...])
        transposed_product()
        grad[k] = place_terms(col_table)
        pair = {}
        for o in far_first + [0]:
            to_z = lax.rem(z + o, n_z)
            pair[o] = remote(
                grad.at[k, p_part(other_core, to_z)], pair_in.at[k, half_part(to_z)],
                pair_send.at[k, o], pair_recv.at[k, o], sibling,
            )
            pair[o].start()
        for o in far_first:
            to_z = lax.rem(z + o, n_z)
            pair[o].wait_recv()
            pair_sum[k, half_part(to_z)] = grad[k, p_part(core, to_z)] + pair_in[k, half_part(to_z)]
            remote(
                pair_sum.at[k, half_part(to_z)], ring_in.at[k, o - 1],
                ring_send.at[k], ring_recv.at[k], (2 * to_z + core, c),
            ).start()
        pair[0].wait_recv()
        gradient = grad[k, own_p] + pair_in[k, half_part(z)]
        whole_ring = remote(ring_in.at[k], ring_in.at[k], ring_send.at[k], ring_recv.at[k], sibling)
        whole_ring.wait_recv()
        for o in range(n_z - 1):
            gradient += ring_in[k, o]

        primal_new[k, own_p] = jnp.clip(primal[own_p] - tau * (cost[own_p] + gradient), 0.0, upper[own_p])
        for o in far_first:
            to_z = lax.rem(z + o, n_z)
            remote(
                primal_new.at[k, own_p], primal_new.at[k, own_p],
                gather_send.at[k], gather_recv.at[k], (2 * to_z + core, c),
            ).start()
        others = primal_new.at[k, pl.ds(0, (n_z - 1) * p_share)]
        whole_gather = remote(others, others, gather_send.at[k], gather_recv.at[k], sibling)
        whole_gather.wait_recv()
        own_half = primal_new.at[k, pl.ds(pl.multiple_of(core * p_half, 8), p_half)]
        half = remote(own_half, own_half, half_send.at[k], half_recv.at[k], sibling)
        half.start()
        half.wait_recv()

        fresh = primal_new[k]
        pick_blocks(col_pick, 2.0 * fresh - primal[...])
        forward_product()
        load[k] = place_terms(row_table)
        for o in range(1, n_col):
            to = lax.rem(c + o, n_col)
            remote(
                load.at[k, d_part(to)], load_in.at[k, o - 1], load_send.at[k], load_recv.at[k], (r, to)
            ).start()

        counter = counter + 1.0
        flag = jnp.where(flag_ref[k] == 1, 1.0, 0.0)
        fresh = primal_new[k]
        step = fresh - primal[...]
        primal_sq[pl.ds(k, 1), :] = jnp.sum(step * step, axis=0, keepdims=True)
        total = sum_primal[...] + fresh
        again = jnp.full((p_rows, LANES), flag) > 0.5
        primal[...] = jnp.where(again, total / jnp.full((p_rows, LANES), counter), fresh)
        sum_primal[...] = jnp.where(again, 0.0, total)

        whole_load = remote(load_in.at[k], load_in.at[k], load_send.at[k], load_recv.at[k], sibling)
        whole_load.wait_recv()
        loaded = load[k, own_d]
        for o in range(n_col - 1):
            loaded += load_in[k, o]
        dual_new[k, own_d] = jnp.maximum(dual[own_d] + sigma * (loaded - cap[own_d]), 0.0)
        for o in range(1, n_col):
            to = lax.rem(c + o, n_col)
            remote(
                dual_new.at[k, own_d], dual_new.at[k, own_d], dual_send.at[k], dual_recv.at[k], (r, to)
            ).start()
        other_d = dual_new.at[k, pl.ds(0, (n_col - 1) * d_share)]
        whole_dual = remote(other_d, other_d, dual_send.at[k], dual_recv.at[k], sibling)
        whole_dual.wait_recv()

        fresh = dual_new[k]
        step = fresh - dual[...]
        dual_sq[pl.ds(k, 1), :] = jnp.sum(step * step, axis=0, keepdims=True)
        total = sum_dual[...] + fresh
        again = jnp.full((d_rows, LANES), flag) > 0.5
        dual[...] = jnp.where(again, total / jnp.full((d_rows, LANES), counter), fresh)
        sum_dual[...] = jnp.where(again, 0.0, total)

        for o in range(n_z):
            pair[o].wait_send()
        whole_ring.wait_send()
        whole_gather.wait_send()
        half.wait_send()
        whole_load.wait_send()
        whole_dual.wait_send()
        return jnp.where(flag_ref[k] == 1, 0.0, counter)

    lax.fori_loop(0, ITERS, iteration, jnp.float32(0.0))

    out_copies = [
        pltpu.make_async_copy(primal, primal_out, out_sem.at[0]),
        pltpu.make_async_copy(dual, dual_out, out_sem.at[1]),
    ]
    for copy in out_copies:
        copy.start()
    for o in range(1, n_row):
        to = lax.rem(r + o, n_row)
        remote(dual_sq, dual_sq_in.at[r], sq_send.at[0], sq_recv.at[0], (to, c)).start()
    for o in range(1, n_col):
        to = lax.rem(c + o, n_col)
        remote(primal_sq, primal_sq_in.at[c], sq_send.at[1], sq_recv.at[1], (r, to)).start()
    dual_sq_in[r] = dual_sq[...]
    primal_sq_in[c] = primal_sq[...]
    for i, (ref, n) in enumerate(((dual_sq_in, n_row), (primal_sq_in, n_col))):
        part = ref.at[pl.ds(0, n - 1)]
        whole = remote(part, part, sq_send.at[i], sq_recv.at[i], sibling)
        whole.wait_recv()
        whole.wait_send()
    p_total = jnp.sum(jnp.sum(primal_sq_in[...], axis=0), axis=1, keepdims=True)
    d_total = jnp.sum(jnp.sum(dual_sq_in[...], axis=0), axis=1, keepdims=True)
    moves = jnp.sqrt(p_total / tau + d_total / sigma + 1e-6)
    for k in range(ITERS):
        move_out[k] = moves[k, 0]
    for copy in out_copies:
        copy.wait()


def shards(n_row, n_col, tiles, tile_row, tile_col, live_count, cost, upper, capacity, step_sizes, restart_flags):
    slots, width = tiles.shape[2], tiles.shape[3]
    p_rows, d_rows = cost.shape[0] // LANES, capacity.shape[0] // LANES
    p_share, d_share, n_z = p_rows // n_row, d_rows // n_col, n_row // 2
    f32, bf16 = jnp.float32, jnp.bfloat16
    vmem, smem, hbm = (pl.BlockSpec(memory_space=m) for m in (pltpu.VMEM, pltpu.SMEM, pl.ANY))
    dma = pltpu.SemaphoreType.DMA
    primal, dual, moves = pl.pallas_call(
        functools.partial(kernel, n_row, n_col),
        out_shape=(
            jax.ShapeDtypeStruct((p_rows, LANES), f32),
            jax.ShapeDtypeStruct((d_rows, LANES), f32),
            jax.ShapeDtypeStruct((ITERS,), f32),
        ),
        in_specs=[hbm, vmem, vmem, hbm, hbm, hbm, smem, smem, smem],
        out_specs=(hbm, hbm, smem),
        scratch_shapes=[
            pltpu.VMEM((slots, width, width), bf16),
            pltpu.VMEM((p_rows, LANES), f32),
            pltpu.VMEM((p_rows, LANES), f32),
            pltpu.VMEM((d_rows, LANES), f32),
            pltpu.VMEM((p_rows, 2 * slots), bf16),
            pltpu.VMEM((2 * slots, p_rows), bf16),
            pltpu.VMEM((d_rows, 2 * slots), bf16),
            pltpu.VMEM((2 * slots, d_rows), bf16),
            pltpu.VMEM((p_rows, LANES), f32),
            pltpu.VMEM((p_rows, LANES), f32),
            pltpu.VMEM((d_rows, LANES), f32),
            pltpu.VMEM((d_rows, LANES), f32),
            pltpu.VMEM((slots, width), bf16),
            pltpu.VMEM((slots, width), f32),
            pltpu.VMEM((ITERS, p_rows, LANES), f32),
            pltpu.VMEM((ITERS, p_rows // 2, LANES), f32),
            pltpu.VMEM((ITERS, p_rows // 2, LANES), f32),
            pltpu.VMEM((ITERS, n_z - 1, p_share, LANES), f32),
            pltpu.VMEM((ITERS, p_rows, LANES), f32),
            pltpu.VMEM((ITERS, d_rows, LANES), f32),
            pltpu.VMEM((ITERS, n_col - 1, d_share, LANES), f32),
            pltpu.VMEM((ITERS, d_rows, LANES), f32),
            pltpu.VMEM((8, LANES), f32),
            pltpu.VMEM((8, LANES), f32),
            pltpu.VMEM((n_col, 8, LANES), f32),
            pltpu.VMEM((n_row, 8, LANES), f32),
            dma((slots // GROUP,)), dma((3,)), dma((2,)),
            dma((ITERS, n_z)), dma((ITERS, n_z)),
            dma((ITERS,)), dma((ITERS,)), dma((ITERS,)), dma((ITERS,)), dma((ITERS,)), dma((ITERS,)),
            dma((ITERS,)), dma((ITERS,)), dma((ITERS,)), dma((ITERS,)), dma((2,)), dma((2,)),
        ],
        compiler_params=pltpu.CompilerParams(
            collective_id=0, has_side_effects=True, vmem_limit_bytes=40 * 2**20
        ),
        name="pdhg",
    )(
        tiles.reshape(slots, width, width),
        tile_col.reshape(1, slots),
        tile_row.reshape(1, slots),
        cost.reshape(p_rows, LANES),
        upper.reshape(p_rows, LANES),
        capacity.reshape(d_rows, LANES),
        live_count,
        step_sizes,
        restart_flags,
    )
    return primal.reshape(-1), dual.reshape(-1), moves


def solution(mesh):
    in_specs = (
        P("row", "col", None, None, None),
        P("row", "col", None),
        P("row", "col", None),
        P("row", "col"),
        P("col"),
        P("col"),
        P("row"),
        P(),
        P(),
    )
    out_specs = (P("col"), P("row"), P())
    body = functools.partial(shards, mesh.shape["row"], mesh.shape["col"])
    return jax.shard_map(body, mesh=mesh, in_specs=in_specs, out_specs=out_specs, check_vma=False)
```

time: 923 us -> 137 us (0.15)
  waiting for transfers between devices: 758 us -> 0 us
  Pallas kernels: 0 us -> 125 us
  blocking collectives: 60.1 us -> 0 us
  matrix products: 44.2 us -> 0 us
  between operations: 28.1 us -> 1.3 us
  other arithmetic: 18 us -> 0 us
    psum x8 -> x0, waiting for transfers between devices: 758 us -> none  [the longest x4 440 us: shards(): gradient = lax.psum(gradient_part, 'row')]
    pallas_call x0 -> x1, Pallas kernels: none -> 125 us  [shards(): pl.pallas_call(functools.partial(kernel, n_row, n_col), out_shape=(jax.Sh...]
    psum x2 -> x0, blocking collectives: 60.1 us -> none  [the longest x1 33.8 us: shards(): primal_square = lax.psum(jnp.sum(primal_step * primal_step), 'col')]
    dot_general x16 -> x0, matrix products: 44.2 us -> none  [the longest x4 22.5 us: forward_terms(): jnp.einsum('tij,tj->ti', tile_set, picked, preferred_element_type=jnp.flo...]
    reduce_sum x4 -> x0, other arithmetic: 9.75 us -> none  [the longest x3 6.95 us: shards(): primal_square = lax.psum(jnp.sum(primal_step * primal_step), 'col')]
  transfers between devices with their start and end apart: 8 -> 0, of which waited for: 8 -> 0; matrix products, arithmetic and copies ran while one was open for 0% -> 0% of each run, Pallas kernels for 0% -> 0%
where the time goes in v1:
time: 137 us
  Pallas kernels  125 us (91%)
  local copies, waits for them, and re-layouts  10.6 us (8%)
    pallas_call x1, Pallas kernels, shards(): pl.pallas_call(functools.partial(kernel, n_row, n_col), out_shape=(jax.Sh...  125 us
    unnamed x19, local copies, waits for them, and re-layouts  10.6 us

profile of v1, /device:TPU:1, one launch (start us, length us, event | category | flops | bytes accessed | tf_op | source)
XLA Modules:
  0.0 136.9 jit_solution(14449841634192823547)
XLA Ops:
  1.3 0.0 copy-start
  1.3 3.4 %copy-done = bf16[1,1,64,256,256]{4,3,2,1,0:T(8,128)(2,1)S(1)} copy-done((bf16[1,1,64,256,256]{4,3,2,1,0:T(8,128)(2,1)S(1)}, bf16[1,1,64,256,256]{4,3,2,1,0:T(8,128)(2,1)}, u32[]{:S(2)}) %copy-start) | copy-done | bytes 8388632
  4.7 0.0 copy-start.1
  4.7 0.9 copy-done.1
  5.6 0.0 copy-start.2
  5.6 0.9 copy-done.2
  6.6 0.0 copy-start.3
  6.6 0.8 copy-done.3
  7.4 0.0 copy-start.4
  7.4 0.7 copy-done.4
  8.1 0.0 copy-start.5
  8.1 0.7 copy-done.5
  8.7 0.0 copy-start.6
  8.7 0.7 copy-done.6
  9.4 0.0 copy-start.7
  9.4 0.7 copy-done.7
  10.0 125.0 %pdhg.1 = (f32[512,128]{1,0:T(8,128)S(1)}, f32[128,128]{1,0:T(8,128)S(1)}, f32[4]{0:T(128)S(1)}) custom-call(bf16[64,256,256]{2,1,0:T(8,128)(2,1)S(1)} %bitcast.8, s32[1,64]{1,0:T(1,128)S(1)} %bitcast.14, s32[1,64]{1,0:T(1,128)S(1)} %bitcast.15, f32[512,128]{1,0:T(8,128)S(1)} %bitcast.9, f32[512,128]{1,0:T(8,128)S(1)} %bitcast.10, f32[128,128]{1,0:T(8,128)S(1)} %bitcast.12, ...), custom_call_target="tpu_custom_call" | custom-call | tf_op jit(solution)/shard_map/pdhg/pallas_call | solution.py:273
  135.0 0.7 copy.16
  135.8 0.6 copy.17
  136.4 0.5 copy.18
Async XLA Ops:
  1.3 3.4 %copy-start = (bf16[1,1,64,256,256]{4,3,2,1,0:T(8,128)(2,1)S(1)}, bf16[1,1,64,256,256]{4,3,2,1,0:T(8,128)(2,1)}, u32[]{:S(2)}) copy-start(bf16[1,1,64,256,256]{4,3,2,1,0:T(8,128)(2,1)} %param.9) | copy-start | bytes 25165828
  4.7 0.9 copy-start.1
  5.6 0.9 copy-start.2
  6.6 0.8 copy-start.3
  7.4 0.7 copy-start.4
  8.1 0.7 copy-start.5
  8.7 0.7 copy-start.6
  9.4 0.7 copy-start.7

commit v2 on v1

v2 whole, which is shorter than its diff:
```python
import functools

import jax
import jax.numpy as jnp
from jax import lax
from jax.experimental import pallas as pl
from jax.experimental.pallas import tpu as pltpu
from jax.sharding import PartitionSpec as P

ITERS = 4
LANES = 128
GROUP = 16
VMEM_LIMIT = 48 * 2**20
MESH = pl.DeviceIdType.MESH


def split(values):
    high = values.astype(jnp.bfloat16)
    rest = values - high.astype(jnp.float32)
    mid = rest.astype(jnp.bfloat16)
    low = (rest - mid.astype(jnp.float32)).astype(jnp.bfloat16)
    return jnp.concatenate([high, mid, low], axis=0)


def kernel(
    n_row, n_col,
    tiles_hbm, col_hbm, row_hbm, cost_hbm, upper_hbm, cap_hbm, step_hbm, flag_hbm, count_ref,
    primal_out, dual_out, move_out,
    tiles, tiles_t, cost, upper, cap, col_index, row_index, step_ref, flag_ref,
    col_table, col_pick, row_table, row_pick,
    primal, sum_primal, dual, sum_dual, primal_done, dual_done, picked, terms,
    grad, pair_in, pair_sum, ring_in, primal_new, x_in, y_in,
    primal_sq, dual_sq, primal_sq_in, dual_sq_in,
    tile_sem, in_sem, out_sem,
    pair_send, pair_recv, ring_send, ring_recv, gather_send, gather_recv, pass_send, pass_recv,
    line_send, x_recv, y_recv, sq_send, sq_recv,
):
    r = lax.axis_index("row")
    c = lax.axis_index("col")
    z, core = lax.div(r, 2), lax.rem(r, 2)
    n_z, n_line = n_row // 2, int(n_col**0.5)
    x, y = lax.div(c, n_line), lax.rem(c, n_line)
    slots, width = tiles.shape[0], tiles.shape[1]
    p_rows, d_rows = primal.shape[0], dual.shape[0]
    p_half, p_share, d_half = p_rows // 2, p_rows // n_row, d_rows // 2
    groups = slots // GROUP
    other = 1 - core
    sibling = (2 * z + other, c)

    def tile_copy(g):
        part = pl.ds(g * GROUP, GROUP)
        return pltpu.make_async_copy(tiles_hbm.at[part], tiles.at[part], tile_sem.at[g])

    own_in = pl.ds(pl.multiple_of(z * 2 * p_share, 8), 2 * p_share)
    in_copies = [
        pltpu.make_async_copy(src, dst, in_sem.at[i])
        for i, (src, dst) in enumerate((
            (col_hbm, col_index), (row_hbm, row_index), (step_hbm, step_ref),
            (flag_hbm, flag_ref), (cost_hbm.at[own_in], cost), (upper_hbm.at[own_in], upper), (cap_hbm, cap),
        ))
    ]
    for copy in in_copies:
        copy.start()
    for g in range(groups):
        tile_copy(g).start()

    barrier = pltpu.get_barrier_semaphore()
    for o in range(1, n_row):
        pl.semaphore_signal(barrier, inc=1, device_id=(lax.rem(r + o, n_row), c), device_id_type=MESH)
    for o in range(1, n_col):
        pl.semaphore_signal(barrier, inc=1, device_id=(r, lax.rem(c + o, n_col)), device_id_type=MESH)

    for ref in (primal, sum_primal, dual, sum_dual, primal_sq, dual_sq):
        ref[...] = jnp.zeros_like(ref)
    for copy in in_copies:
        copy.wait()

    lane = lax.broadcasted_iota(jnp.int32, (1, 3 * slots), 1)
    live = lax.rem(lane, slots) < count_ref[0, 0]

    def tables(index_ref, n_blocks, table, pick):
        index = index_ref[...]
        key = jnp.where(live, jnp.concatenate([index, index, index], axis=1), -1)
        hot = jnp.where(lax.broadcasted_iota(jnp.int32, (n_blocks, 3 * slots), 0) == key, 1.0, 0.0)
        table[...] = hot.astype(jnp.bfloat16)
        pick[...] = hot[:, :slots].T.astype(jnp.bfloat16)

    tables(row_index, d_half, row_table, row_pick)
    tables(col_index, p_half, col_table, col_pick)
    tau, sigma = step_ref[0], step_ref[1]

    def deal(ref, rows):
        return ref[pl.ds(0, rows, stride=2), :], ref[pl.ds(1, rows, stride=2), :]

    def weave(ref, out):
        rows = ref.shape[0] // 2
        out[pl.ds(0, rows, stride=2), :] = ref[:rows]
        out[pl.ds(1, rows, stride=2), :] = ref[rows:]

    first = jnp.full((p_share, LANES), core) == 0
    own_cost = jnp.where(first, *deal(cost, p_share))
    own_upper = jnp.where(first, *deal(upper, p_share))
    capacity = jnp.concatenate(deal(cap, d_half), axis=0)
    for g in range(groups):
        tile_copy(g).wait()

    def half_lanes(h):
        return pl.ds(pl.multiple_of(h * LANES, LANES), LANES)

    def pick_blocks(pick, values, h):
        chosen = jnp.dot(pick[...], values.astype(jnp.bfloat16), preferred_element_type=jnp.float32)
        picked[:, half_lanes(h)] = chosen.astype(jnp.bfloat16)

    def diagonal(values):
        depth = values.shape[1]
        at_row = lax.broadcasted_iota(jnp.int32, (GROUP, GROUP * depth), 0)
        at_tile = lax.div(lax.broadcasted_iota(jnp.int32, (GROUP, GROUP * depth), 1), depth)
        wide = jnp.concatenate([values] * GROUP, axis=1)
        return jnp.where(at_row == at_tile, wide, jnp.zeros((), jnp.bfloat16))

    def group_part(g):
        return pl.ds(g * GROUP, GROUP)

    def transposed_half(h):
        for g in range(groups):
            part = group_part(g)
            right = tiles[part, :, half_lanes(h)].reshape(GROUP * width, LANES)
            terms[part, :LANES] = jnp.dot(diagonal(picked[part, :]), right, preferred_element_type=jnp.float32)
        return jnp.dot(col_table[...], split(terms[:, :LANES]), preferred_element_type=jnp.float32)

    def forward_half(h, add):
        depth = pl.ds(pl.multiple_of(h * LANES, LANES), LANES)
        for g in range(groups):
            part = group_part(g)
            right = tiles_t[part, depth, :].reshape(GROUP * LANES, width)
            some = jnp.dot(diagonal(picked[part, half_lanes(h)]), right, preferred_element_type=jnp.float32)
            terms[part, :] = terms[part, :] + some if add else some

    def transpose_tiles():
        def four(i, _):
            for s in range(4):
                tiles_t[4 * i + s] = tiles[4 * i + s].T
            return 0

        lax.fori_loop(0, slots // 4, four, 0)

    def half_part(h):
        return pl.ds(pl.multiple_of(h * p_half, 8), p_half)

    def z_part(which_z):
        return pl.ds(pl.multiple_of(which_z * p_share, 8), p_share)

    def p_part(h, which_z):
        return pl.ds(pl.multiple_of(h * p_half + which_z * p_share, 8), p_share)

    def remote(src, dst, send, recv, device):
        return pltpu.make_async_remote_copy(
            src_ref=src, dst_ref=dst, send_sem=send, recv_sem=recv, device_id=device, device_id_type=MESH
        )

    def at_z(o):
        return (2 * lax.rem(z + o, n_z) + core, c)

    near_first = sorted(range(1, n_z), key=lambda o: min(o, n_z - o))
    far_first = near_first[::-1]
    own_p = p_part(core, z)
    x_peers = [(r, lax.rem(x + o, n_line) * n_line + y) for o in range(1, n_line)]
    y_peers = [(r, x * n_line + lax.rem(y + o, n_line)) for o in range(1, n_line)]

    def sum_lines(ref, k, phase):
        total = ref[k, phase, 0]
        for i in range(1, n_line):
            total += ref[k, phase, i]
        return total

    def start_x(k, phase):
        for peer in x_peers:
            remote(x_in.at[k, phase, x], x_in.at[k, phase, x], line_send.at[k], x_recv.at[k, phase], peer).start()

    def start_y(k, phase):
        for peer in y_peers:
            remote(y_in.at[k, phase, y], y_in.at[k, phase, y], line_send.at[k], y_recv.at[k, phase], peer).start()

    def wait_line(ref, sem, k, phase):
        part = ref.at[k, phase, pl.ds(0, n_line - 1)]
        remote(part, part, line_send.at[k], sem.at[k, phase], sibling).wait_recv()

    def send_squares(ref, ref_in, i, me, n, device):
        ref_in[me] = ref[...]
        for o in range(1, n):
            to = lax.rem(me + o, n)
            remote(ref, ref_in.at[me], sq_send.at[i], sq_recv.at[i], device(to)).start()

    def gradient_step(k):
        for h in range(2):
            pick_blocks(row_pick, dual[h * d_half:(h + 1) * d_half], h)
        grad[k, half_part(other)] = transposed_half(other)

        @pl.when(k == 0)
        def _():
            pl.semaphore_wait(barrier, n_row - 1 + n_col - 1)

        pair = {}
        for o in far_first + [0]:
            to_z = lax.rem(z + o, n_z)
            pair[o] = remote(
                grad.at[k, p_part(other, to_z)], pair_in.at[k, z_part(to_z)],
                pair_send.at[k], pair_recv.at[k, o], sibling,
            )
            pair[o].start()
        grad[k, half_part(core)] = transposed_half(core)
        for o in far_first:
            to_z = lax.rem(z + o, n_z)
            pair[o].wait_recv()
            pair_sum[k, z_part(to_z)] = grad[k, p_part(core, to_z)] + pair_in[k, z_part(to_z)]
            remote(
                pair_sum.at[k, z_part(to_z)], ring_in.at[k, o - 1], ring_send.at[k], ring_recv.at[k], at_z(o)
            ).start()
        pair[0].wait_recv()
        gradient = grad[k, own_p] + pair_in[k, z_part(z)]

        @pl.when(k == 0)
        def _():
            transpose_tiles()

        remote(ring_in.at[k], ring_in.at[k], ring_send.at[k], ring_recv.at[k], sibling).wait_recv()
        for i in range(n_z - 1):
            gradient += ring_in[k, i]

        primal_new[k, own_p] = jnp.clip(primal[own_p] - tau * (own_cost + gradient), 0.0, own_upper)
        mine = primal_new.at[k, own_p]
        for o in far_first:
            remote(mine, mine, gather_send.at[k], gather_recv.at[k, o], at_z(o)).start()
        remote(mine, mine, pass_send.at[k], pass_recv.at[k], sibling).start()
        for o in near_first:
            here = primal_new.at[k, p_part(core, lax.rem(z + n_z - o, n_z))]
            remote(here, here, gather_send.at[k], gather_recv.at[k, o], sibling).wait_recv()
            remote(here, here, pass_send.at[k], pass_recv.at[k], sibling).start()

    def extrapolated(k, h):
        return 2.0 * primal_new[k, half_part(h)] - primal[half_part(h)]

    def load_step(k, counter):
        pick_blocks(col_pick, extrapolated(k, core), core)
        forward_half(core, False)
        passed = primal_new.at[k, half_part(core)]
        remote(passed, passed, pass_send.at[k], pass_recv.at[k], sibling).wait_recv()
        pick_blocks(col_pick, extrapolated(k, other), other)
        forward_half(other, True)

        x_in[k, 0, x] = jnp.dot(row_table[...], split(terms[:, :LANES]), preferred_element_type=jnp.float32)
        start_x(k, 0)
        y_in[k, 0, y] = jnp.dot(row_table[...], split(terms[:, LANES:]), preferred_element_type=jnp.float32)
        start_y(k, 0)

        counter = counter + 1.0
        flag = jnp.where(flag_ref[k] == 1, 1.0, 0.0)
        fresh = primal_new[k]
        step = fresh - primal[...]
        primal_sq[pl.ds(k, 1), :] = jnp.sum(step * step, axis=0, keepdims=True)
        total = sum_primal[...] + fresh
        again = jnp.full((p_rows, LANES), flag) > 0.5
        primal[...] = jnp.where(again, total / jnp.full((p_rows, LANES), counter), fresh)
        sum_primal[...] = jnp.where(again, 0.0, total)

        wait_line(x_in, x_recv, k, 0)
        y_in[k, 1, y] = sum_lines(x_in, k, 0)
        start_y(k, 1)
        wait_line(y_in, y_recv, k, 0)
        x_in[k, 1, x] = sum_lines(y_in, k, 0)
        start_x(k, 1)

        @pl.when(k == ITERS - 1)
        def _():
            send_squares(primal_sq, primal_sq_in, 1, c, n_col, lambda to: (r, to))
            weave(primal, primal_done)
            pltpu.make_async_copy(primal_done, primal_out, out_sem.at[0]).start()

        wait_line(y_in, y_recv, k, 1)
        wait_line(x_in, x_recv, k, 1)
        loaded = jnp.concatenate([sum_lines(y_in, k, 1), sum_lines(x_in, k, 1)], axis=0)
        old = dual[...]
        fresh = jnp.maximum(old + sigma * (loaded - capacity), 0.0)
        step = fresh - old
        dual_sq[pl.ds(k, 1), :] = jnp.sum(step * step, axis=0, keepdims=True)
        total = sum_dual[...] + fresh
        again = jnp.full((d_rows, LANES), flag) > 0.5
        dual[...] = jnp.where(again, total / jnp.full((d_rows, LANES), counter), fresh)
        sum_dual[...] = jnp.where(again, 0.0, total)
        return jnp.where(flag_ref[k] == 1, 0.0, counter)

    def iteration(k, counter):
        gradient_step(k)
        return load_step(k, counter)

    lax.fori_loop(0, ITERS, iteration, jnp.float32(0.0))

    send_squares(dual_sq, dual_sq_in, 0, r, n_row, lambda to: (to, c))
    weave(dual, dual_done)
    dual_copy = pltpu.make_async_copy(dual_done, dual_out, out_sem.at[1])
    dual_copy.start()

    def sent(k, _):
        def wait(ref, sem):
            remote(ref, ref, sem.at[k], sem.at[k], sibling).wait_send()

        wait(grad.at[k, pl.ds(0, n_z * p_share)], pair_send)
        wait(grad.at[k, pl.ds(0, (n_z - 1) * p_share)], ring_send)
        wait(grad.at[k, pl.ds(0, (n_z - 1) * p_share)], gather_send)
        wait(grad.at[k, pl.ds(0, n_z * p_share)], pass_send)
        for _ in range(2):
            wait(x_in.at[k, 0, pl.ds(0, n_line - 1)], line_send)
            wait(y_in.at[k, 0, pl.ds(0, n_line - 1)], line_send)
        return 0

    lax.fori_loop(0, ITERS, sent, 0)
    for i, (ref, n) in enumerate(((dual_sq_in, n_row), (primal_sq_in, n_col))):
        part = ref.at[pl.ds(0, n - 1)]
        whole = remote(part, part, sq_send.at[i], sq_recv.at[i], sibling)
        whole.wait_send()
        whole.wait_recv()
    p_total = jnp.sum(jnp.sum(primal_sq_in[...], axis=0), axis=1, keepdims=True)
    d_total = jnp.sum(jnp.sum(dual_sq_in[...], axis=0), axis=1, keepdims=True)
    moves = jnp.sqrt(p_total / tau + d_total / sigma + 1e-6)
    for k in range(ITERS):
        move_out[k] = moves[k, 0]
    pltpu.make_async_copy(primal_done, primal_out, out_sem.at[0]).wait()
    dual_copy.wait()


def shards(n_row, n_col, tiles, tile_row, tile_col, live_count, cost, upper, capacity, step_sizes, restart_flags):
    slots, width = tiles.shape[2], tiles.shape[3]
    p_rows, d_rows = cost.shape[0] // LANES, capacity.shape[0] // LANES
    p_share, n_z, n_line = p_rows // n_row, n_row // 2, int(n_col**0.5)
    f32, bf16, i32 = jnp.float32, jnp.bfloat16, jnp.int32
    hbm = pl.BlockSpec(memory_space=pltpu.HBM)
    anywhere = pl.BlockSpec(memory_space=pl.ANY)
    smem = pl.BlockSpec(memory_space=pltpu.SMEM)
    dma = pltpu.SemaphoreType.DMA
    out_shape = (
        jax.ShapeDtypeStruct((p_rows, LANES), f32),
        jax.ShapeDtypeStruct((d_rows, LANES), f32),
        jax.ShapeDtypeStruct((ITERS,), f32),
    )
    primal, dual, moves = pl.pallas_call(
        functools.partial(kernel, n_row, n_col),
        out_shape=out_shape,
        in_specs=[hbm] * 8 + [smem],
        out_specs=(anywhere, anywhere, smem),
        scratch_shapes=[
            pltpu.VMEM((slots, width, width), bf16),
            pltpu.VMEM((slots, width, width), bf16),
            pltpu.VMEM((2 * p_share, LANES), f32),
            pltpu.VMEM((2 * p_share, LANES), f32),
            pltpu.VMEM((d_rows, LANES), f32),
            pltpu.VMEM((1, slots), i32),
            pltpu.VMEM((1, slots), i32),
            pltpu.SMEM((2,), f32),
            pltpu.SMEM((ITERS,), i32),
            pltpu.VMEM((p_rows // 2, 3 * slots), bf16),
            pltpu.VMEM((slots, p_rows // 2), bf16),
            pltpu.VMEM((d_rows // 2, 3 * slots), bf16),
            pltpu.VMEM((slots, d_rows // 2), bf16),
            pltpu.VMEM((p_rows, LANES), f32),
            pltpu.VMEM((p_rows, LANES), f32),
            pltpu.VMEM((d_rows, LANES), f32),
            pltpu.VMEM((d_rows, LANES), f32),
            pltpu.VMEM((p_rows, LANES), f32),
            pltpu.VMEM((d_rows, LANES), f32),
            pltpu.VMEM((slots, width), bf16),
            pltpu.VMEM((slots, width), f32),
            pltpu.VMEM((ITERS, p_rows, LANES), f32),
            pltpu.VMEM((ITERS, p_rows // 2, LANES), f32),
            pltpu.VMEM((ITERS, p_rows // 2, LANES), f32),
            pltpu.VMEM((ITERS, n_z - 1, p_share, LANES), f32),
            pltpu.VMEM((ITERS, p_rows, LANES), f32),
            pltpu.VMEM((ITERS, 2, n_line, d_rows // 2, LANES), f32),
            pltpu.VMEM((ITERS, 2, n_line, d_rows // 2, LANES), f32),
            pltpu.VMEM((8, LANES), f32),
            pltpu.VMEM((8, LANES), f32),
            pltpu.VMEM((n_col, 8, LANES), f32),
            pltpu.VMEM((n_row, 8, LANES), f32),
            dma((slots // GROUP,)), dma((7,)), dma((2,)),
            dma((ITERS,)), dma((ITERS, n_z)), dma((ITERS,)), dma((ITERS,)),
            dma((ITERS,)), dma((ITERS, n_z)), dma((ITERS,)), dma((ITERS,)),
            dma((ITERS,)), dma((ITERS, 2)), dma((ITERS, 2)), dma((2,)), dma((2,)),
        ],
        compiler_params=pltpu.CompilerParams(
            collective_id=0, has_side_effects=True, vmem_limit_bytes=VMEM_LIMIT
        ),
        name="pdhg",
    )(
        *(
            pltpu.with_memory_space_constraint(operand, pltpu.HBM)
            for operand in (
                tiles.reshape(slots, width, width),
                tile_col.reshape(1, slots),
                tile_row.reshape(1, slots),
                cost.reshape(p_rows, LANES),
                upper.reshape(p_rows, LANES),
                capacity.reshape(d_rows, LANES),
                step_sizes,
                restart_flags,
            )
        ),
        live_count,
    )
    return primal.reshape(-1), dual.reshape(-1), moves


def solution(mesh):
    in_specs = (
        P("row", "col", None, None, None),
        P("row", "col", None),
        P("row", "col", None),
        P("row", "col"),
        P("col"),
        P("col"),
        P("row"),
        P(),
        P(),
    )
    out_specs = (P("col"), P("row"), P())
    body = functools.partial(shards, mesh.shape["row"], mesh.shape["col"])
    return jax.shard_map(body, mesh=mesh, in_specs=in_specs, out_specs=out_specs, check_vma=False)
```

time: 137 us -> 114 us (0.83)
  Pallas kernels: 125 us -> 111 us
  local copies, waits for them, and re-layouts: 10.6 us -> 1.87 us
    pallas_call x1, Pallas kernels: 125 us -> 111 us  [shards(): pl.pallas_call(functools.partial(kernel, n_row, n_col), out_shape=out_sha...]
    unnamed x19 -> x3, local copies, waits for them, and re-layouts: 10.6 us -> 1.87 us
where the time goes in v2:
time: 114 us
  Pallas kernels  111 us (97%)
  local copies, waits for them, and re-layouts  1.87 us (2%)
  between operations  1.29 us (1%)
    pallas_call x1, Pallas kernels, shards(): pl.pallas_call(functools.partial(kernel, n_row, n_col), out_shape=out_sha...  111 us

profile of v2, /device:TPU:1, one launch (start us, length us, event | category | flops | bytes accessed | tf_op | source)
XLA Modules:
  0.0 114.2 jit_solution(14979141544952437009)
XLA Ops:
  1.3 111.0 %pdhg.1 = (f32[512,128]{1,0:T(8,128)S(1)}, f32[128,128]{1,0:T(8,128)S(1)}, f32[4]{0:T(128)S(1)}) custom-call(bf16[64,256,256]{2,1,0:T(8,128)(2,1)} %bitcast.10, s32[1,64]{1,0:T(1,128)} %bitcast.14, s32[1,64]{1,0:T(1,128)} %bitcast.15, f32[512,128]{1,0:T(8,128)} %bitcast.11, f32[512,128]{1,0:T(8,128)} %bitcast.12, f32[128,128]{1,0:T(8,128)} %bitcast.13, ...), custom_call_target="tpu_custom_call" | custom-call | tf_op jit(solution)/shard_map/pdhg/pallas_call | solution.py:345
  112.3 0.7 copy.16
  113.1 0.6 copy.17
  113.7 0.5 copy.18

commit v3 on v2

--- a/solution.py
+++ b/solution.py
@@ -26,7 +26,7 @@
     n_row, n_col,
     tiles_hbm, col_hbm, row_hbm, cost_hbm, upper_hbm, cap_hbm, step_hbm, flag_hbm, count_ref,
     primal_out, dual_out, move_out,
-    tiles, tiles_t, cost, upper, cap, col_index, row_index, step_ref, flag_ref,
+    tiles, tiles_t, cost_in, upper_in, cost, upper, cap, col_index, row_index, step_ref, flag_ref,
     col_table, col_pick, row_table, row_pick,
     primal, sum_primal, dual, sum_dual, primal_done, dual_done, picked, terms,
     grad, pair_in, pair_sum, ring_in, primal_new, x_in, y_in,
@@ -51,12 +51,11 @@
         part = pl.ds(g * GROUP, GROUP)
         return pltpu.make_async_copy(tiles_hbm.at[part], tiles.at[part], tile_sem.at[g])
 
-    own_in = pl.ds(pl.multiple_of(z * 2 * p_share, 8), 2 * p_share)
     in_copies = [
         pltpu.make_async_copy(src, dst, in_sem.at[i])
         for i, (src, dst) in enumerate((
             (col_hbm, col_index), (row_hbm, row_index), (step_hbm, step_ref),
-            (flag_hbm, flag_ref), (cost_hbm.at[own_in], cost), (upper_hbm.at[own_in], upper), (cap_hbm, cap),
+            (flag_hbm, flag_ref), (cost_hbm, cost_in), (upper_hbm, upper_in), (cap_hbm, cap),
         ))
     ]
     for copy in in_copies:
@@ -65,12 +64,12 @@
         tile_copy(g).start()
 
     barrier = pltpu.get_barrier_semaphore()
-    for o in range(1, n_row):
+    for o in sorted(range(1, n_row), key=lambda o: -min(o, n_row - o)):
         pl.semaphore_signal(barrier, inc=1, device_id=(lax.rem(r + o, n_row), c), device_id_type=MESH)
     for o in range(1, n_col):
         pl.semaphore_signal(barrier, inc=1, device_id=(r, lax.rem(c + o, n_col)), device_id_type=MESH)
 
-    for ref in (primal, sum_primal, dual, sum_dual, primal_sq, dual_sq):
+    for ref in (primal_sq, dual_sq):
         ref[...] = jnp.zeros_like(ref)
     for copy in in_copies:
         copy.wait()
@@ -97,12 +96,9 @@
         out[pl.ds(0, rows, stride=2), :] = ref[:rows]
         out[pl.ds(1, rows, stride=2), :] = ref[rows:]
 
-    first = jnp.full((p_share, LANES), core) == 0
-    own_cost = jnp.where(first, *deal(cost, p_share))
-    own_upper = jnp.where(first, *deal(upper, p_share))
+    for dealt, ref in ((cost, cost_in), (upper, upper_in)):
+        dealt[:p_half], dealt[p_half:] = deal(ref, p_half)
     capacity = jnp.concatenate(deal(cap, d_half), axis=0)
-    for g in range(groups):
-        tile_copy(g).wait()
 
     def half_lanes(h):
         return pl.ds(pl.multiple_of(h * LANES, LANES), LANES)
@@ -122,11 +118,12 @@
         return pl.ds(g * GROUP, GROUP)
 
     def transposed_half(h):
+        some = []
         for g in range(groups):
             part = group_part(g)
             right = tiles[part, :, half_lanes(h)].reshape(GROUP * width, LANES)
-            terms[part, :LANES] = jnp.dot(diagonal(picked[part, :]), right, preferred_element_type=jnp.float32)
-        return jnp.dot(col_table[...], split(terms[:, :LANES]), preferred_element_type=jnp.float32)
+            some.append(jnp.dot(diagonal(picked[part, :]), right, preferred_element_type=jnp.float32))
+        return jnp.dot(col_table[...], split(jnp.concatenate(some, axis=0)), preferred_element_type=jnp.float32)
 
     def forward_half(h, add):
         depth = pl.ds(pl.multiple_of(h * LANES, LANES), LANES)
@@ -136,13 +133,27 @@
             some = jnp.dot(diagonal(picked[part, half_lanes(h)]), right, preferred_element_type=jnp.float32)
             terms[part, :] = terms[part, :] + some if add else some
 
-    def transpose_tiles():
+    def forward_early():
+        at_row = lax.broadcasted_iota(jnp.int32, (GROUP, width), 0)
+        for g in range(groups):
+            tile_copy(g).wait()
+            part = group_part(g)
+            mine = picked[part, :]
+            total = jnp.zeros((GROUP, width), jnp.float32)
+            for s in range(GROUP):
+                left = jnp.where(at_row == s, mine, jnp.zeros((), jnp.bfloat16))
+                total += lax.dot_general(
+                    left, tiles[g * GROUP + s], (((1,), (1,)), ((), ())), preferred_element_type=jnp.float32
+                )
+            terms[part, :] = total
+
+    def transpose_tiles(begin, end):
         def four(i, _):
             for s in range(4):
                 tiles_t[4 * i + s] = tiles[4 * i + s].T
             return 0
 
-        lax.fori_loop(0, slots // 4, four, 0)
+        lax.fori_loop(begin // 4, end // 4, four, 0)
 
     def half_part(h):
         return pl.ds(pl.multiple_of(h * p_half, 8), p_half)
@@ -164,8 +175,9 @@
     near_first = sorted(range(1, n_z), key=lambda o: min(o, n_z - o))
     far_first = near_first[::-1]
     own_p = p_part(core, z)
-    x_peers = [(r, lax.rem(x + o, n_line) * n_line + y) for o in range(1, n_line)]
-    y_peers = [(r, x * n_line + lax.rem(y + o, n_line)) for o in range(1, n_line)]
+    far_on_line = sorted(range(1, n_line), key=lambda o: -min(o, n_line - o))
+    x_peers = [(r, lax.rem(x + o, n_line) * n_line + y) for o in far_on_line]
+    y_peers = [(r, x * n_line + lax.rem(y + o, n_line)) for o in far_on_line]
 
     def sum_lines(ref, k, phase):
         total = ref[k, phase, 0]
@@ -187,7 +199,7 @@
 
     def send_squares(ref, ref_in, i, me, n, device):
         ref_in[me] = ref[...]
-        for o in range(1, n):
+        for o in sorted(range(1, n), key=lambda o: -min(o, n - o)):
             to = lax.rem(me + o, n)
             remote(ref, ref_in.at[me], sq_send.at[i], sq_recv.at[i], device(to)).start()
 
@@ -195,11 +207,6 @@
         for h in range(2):
             pick_blocks(row_pick, dual[h * d_half:(h + 1) * d_half], h)
         grad[k, half_part(other)] = transposed_half(other)
-
-        @pl.when(k == 0)
-        def _():
-            pl.semaphore_wait(barrier, n_row - 1 + n_col - 1)
-
         pair = {}
         for o in far_first + [0]:
             to_z = lax.rem(z + o, n_z)
@@ -218,16 +225,11 @@
             ).start()
         pair[0].wait_recv()
         gradient = grad[k, own_p] + pair_in[k, z_part(z)]
-
-        @pl.when(k == 0)
-        def _():
-            transpose_tiles()
-
         remote(ring_in.at[k], ring_in.at[k], ring_send.at[k], ring_recv.at[k], sibling).wait_recv()
         for i in range(n_z - 1):
             gradient += ring_in[k, i]
 
-        primal_new[k, own_p] = jnp.clip(primal[own_p] - tau * (own_cost + gradient), 0.0, own_upper)
+        primal_new[k, own_p] = jnp.clip(primal[own_p] - tau * (cost[own_p] + gradient), 0.0, upper[own_p])
         mine = primal_new.at[k, own_p]
         for o in far_first:
             remote(mine, mine, gather_send.at[k], gather_recv.at[k, o], at_z(o)).start()
@@ -240,7 +242,7 @@
     def extrapolated(k, h):
         return 2.0 * primal_new[k, half_part(h)] - primal[half_part(h)]
 
-    def load_step(k, counter):
+    def forward(k):
         pick_blocks(col_pick, extrapolated(k, core), core)
         forward_half(core, False)
         passed = primal_new.at[k, half_part(core)]
@@ -248,6 +250,7 @@
         pick_blocks(col_pick, extrapolated(k, other), other)
         forward_half(other, True)
 
+    def load_step(k, counter, begin):
         x_in[k, 0, x] = jnp.dot(row_table[...], split(terms[:, :LANES]), preferred_element_type=jnp.float32)
         start_x(k, 0)
         y_in[k, 0, y] = jnp.dot(row_table[...], split(terms[:, LANES:]), preferred_element_type=jnp.float32)
@@ -257,6 +260,8 @@
         flag = jnp.where(flag_ref[k] == 1, 1.0, 0.0)
         fresh = primal_new[k]
         step = fresh - primal[...]
+        if begin:
+            transpose_tiles(0, slots // 2)
         primal_sq[pl.ds(k, 1), :] = jnp.sum(step * step, axis=0, keepdims=True)
         total = sum_primal[...] + fresh
         again = jnp.full((p_rows, LANES), flag) > 0.5
@@ -269,6 +274,8 @@
         wait_line(y_in, y_recv, k, 0)
         x_in[k, 1, x] = sum_lines(y_in, k, 0)
         start_x(k, 1)
+        if begin:
+            transpose_tiles(slots // 2, slots)
 
         @pl.when(k == ITERS - 1)
         def _():
@@ -289,31 +296,45 @@
         sum_dual[...] = jnp.where(again, 0.0, total)
         return jnp.where(flag_ref[k] == 1, 0.0, counter)
 
+    for ref in (primal, sum_primal, dual, sum_dual):
+        ref[...] = jnp.zeros_like(ref)
+    gradient_at_zero = 0.0
+    primal_new[0] = jnp.clip(primal[...] - tau * (cost[...] + gradient_at_zero), 0.0, upper[...])
+    for h in range(2):
+        pick_blocks(col_pick, extrapolated(0, h), h)
+    forward_early()
+    pl.semaphore_wait(barrier, n_row - 1 + n_col - 1)
+    counter = load_step(0, jnp.float32(0.0), True)
+
     def iteration(k, counter):
         gradient_step(k)
-        return load_step(k, counter)
-
-    lax.fori_loop(0, ITERS, iteration, jnp.float32(0.0))
+        forward(k)
+        return load_step(k, counter, False)
+
+    lax.fori_loop(1, ITERS, iteration, counter)
 
     send_squares(dual_sq, dual_sq_in, 0, r, n_row, lambda to: (to, c))
     weave(dual, dual_done)
     dual_copy = pltpu.make_async_copy(dual_done, dual_out, out_sem.at[1])
     dual_copy.start()
 
-    def sent(k, _):
+    def sent(k, _, begin=False):
         def wait(ref, sem):
             remote(ref, ref, sem.at[k], sem.at[k], sibling).wait_send()
 
+        for _ in range(2):
+            wait(x_in.at[k, 0, pl.ds(0, n_line - 1)], line_send)
+            wait(y_in.at[k, 0, pl.ds(0, n_line - 1)], line_send)
+        if begin:
+            return 0
         wait(grad.at[k, pl.ds(0, n_z * p_share)], pair_send)
         wait(grad.at[k, pl.ds(0, (n_z - 1) * p_share)], ring_send)
         wait(grad.at[k, pl.ds(0, (n_z - 1) * p_share)], gather_send)
         wait(grad.at[k, pl.ds(0, n_z * p_share)], pass_send)
-        for _ in range(2):
-            wait(x_in.at[k, 0, pl.ds(0, n_line - 1)], line_send)
-            wait(y_in.at[k, 0, pl.ds(0, n_line - 1)], line_send)
         return 0
 
-    lax.fori_loop(0, ITERS, sent, 0)
+    sent(0, 0, True)
+    lax.fori_loop(1, ITERS, sent, 0)
     for i, (ref, n) in enumerate(((dual_sq_in, n_row), (primal_sq_in, n_col))):
         part = ref.at[pl.ds(0, n - 1)]
         whole = remote(part, part, sq_send.at[i], sq_recv.at[i], sibling)
@@ -322,8 +343,7 @@
     p_total = jnp.sum(jnp.sum(primal_sq_in[...], axis=0), axis=1, keepdims=True)
     d_total = jnp.sum(jnp.sum(dual_sq_in[...], axis=0), axis=1, keepdims=True)
     moves = jnp.sqrt(p_total / tau + d_total / sigma + 1e-6)
-    for k in range(ITERS):
-        move_out[k] = moves[k, 0]
+    move_out[...] = jnp.broadcast_to(moves, move_out.shape)
     pltpu.make_async_copy(primal_done, primal_out, out_sem.at[0]).wait()
     dual_copy.wait()
 
@@ -340,18 +360,20 @@
     out_shape = (
         jax.ShapeDtypeStruct((p_rows, LANES), f32),
         jax.ShapeDtypeStruct((d_rows, LANES), f32),
-        jax.ShapeDtypeStruct((ITERS,), f32),
+        jax.ShapeDtypeStruct((8, LANES), f32),
     )
     primal, dual, moves = pl.pallas_call(
         functools.partial(kernel, n_row, n_col),
         out_shape=out_shape,
         in_specs=[hbm] * 8 + [smem],
-        out_specs=(anywhere, anywhere, smem),
+        out_specs=(anywhere, anywhere, pl.BlockSpec(memory_space=pltpu.VMEM)),
         scratch_shapes=[
             pltpu.VMEM((slots, width, width), bf16),
             pltpu.VMEM((slots, width, width), bf16),
-            pltpu.VMEM((2 * p_share, LANES), f32),
-            pltpu.VMEM((2 * p_share, LANES), f32),
+            pltpu.VMEM((p_rows, LANES), f32),
+            pltpu.VMEM((p_rows, LANES), f32),
+            pltpu.VMEM((p_rows, LANES), f32),
+            pltpu.VMEM((p_rows, LANES), f32),
             pltpu.VMEM((d_rows, LANES), f32),
             pltpu.VMEM((1, slots), i32),
             pltpu.VMEM((1, slots), i32),
@@ -405,7 +427,7 @@
         ),
         live_count,
     )
-    return primal.reshape(-1), dual.reshape(-1), moves
+    return primal.reshape(-1), dual.reshape(-1), moves[:ITERS, 0]
 
 
 def solution(mesh):

time: 114 us -> 101 us (0.89)
  Pallas kernels: 111 us -> 97.8 us
    pallas_call x1, Pallas kernels: 111 us -> 97.8 us  [shards(): pl.pallas_call(functools.partial(kernel, n_row, n_col), out_shape=out_sha...]
where the time goes in v3:
time: 101 us
  Pallas kernels  97.8 us (97%)
  local copies, waits for them, and re-layouts  1.98 us (2%)
  between operations  1.29 us (1%)
    pallas_call x1, Pallas kernels, shards(): pl.pallas_call(functools.partial(kernel, n_row, n_col), out_shape=out_sha...  97.8 us

profile of v3, /device:TPU:1, one launch (start us, length us, event | category | flops | bytes accessed | tf_op | source)
XLA Modules:
  0.0 101.1 jit_solution(11236763491794999232)
XLA Ops:
  1.3 97.8 %pdhg.1 = (f32[512,128]{1,0:T(8,128)S(1)}, f32[128,128]{1,0:T(8,128)S(1)}, f32[8,128]{1,0:T(8,128)S(1)}) custom-call(bf16[64,256,256]{2,1,0:T(8,128)(2,1)} %bitcast.10, s32[1,64]{1,0:T(1,128)} %bitcast.14, s32[1,64]{1,0:T(1,128)} %bitcast.15, f32[512,128]{1,0:T(8,128)} %bitcast.11, f32[512,128]{1,0:T(8,128)} %bitcast.12, f32[128,128]{1,0:T(8,128)} %bitcast.13, ...), custom_call_target="tpu_custom_call" | custom-call | tf_op jit(solution)/shard_map/pdhg/pallas_call | solution.py:365
  99.1 0.6 slice_reduce_fusion
  99.8 0.7 copy.15
  100.5 0.6 copy.16

commit v4 on v3

--- a/solution.py
+++ b/solution.py
@@ -64,10 +64,16 @@
         tile_copy(g).start()
 
     barrier = pltpu.get_barrier_semaphore()
-    for o in sorted(range(1, n_row), key=lambda o: -min(o, n_row - o)):
-        pl.semaphore_signal(barrier, inc=1, device_id=(lax.rem(r + o, n_row), c), device_id_type=MESH)
-    for o in range(1, n_col):
-        pl.semaphore_signal(barrier, inc=1, device_id=(r, lax.rem(c + o, n_col)), device_id_type=MESH)
+    def greet(me, n, device):
+        def one(i, _):
+            to = device(lax.rem(me + 1 + i, n))
+            pl.semaphore_signal(barrier, inc=1, device_id=to, device_id_type=MESH)
+            return 0
+
+        lax.fori_loop(0, n - 1, one, 0)
+
+    greet(r, n_row, lambda to: (to, c))
+    greet(c, n_col, lambda to: (r, to))
 
     for ref in (primal_sq, dual_sq):
         ref[...] = jnp.zeros_like(ref)
@@ -135,9 +141,10 @@
 
     def forward_early():
         at_row = lax.broadcasted_iota(jnp.int32, (GROUP, width), 0)
-        for g in range(groups):
+
+        def one(g, _):
             tile_copy(g).wait()
-            part = group_part(g)
+            part = pl.ds(pl.multiple_of(g * GROUP, GROUP), GROUP)
             mine = picked[part, :]
             total = jnp.zeros((GROUP, width), jnp.float32)
             for s in range(GROUP):
@@ -146,6 +153,9 @@
                     left, tiles[g * GROUP + s], (((1,), (1,)), ((), ())), preferred_element_type=jnp.float32
                 )
             terms[part, :] = total
+            return 0
+
+        lax.fori_loop(0, groups, one, 0)
 
     def transpose_tiles(begin, end):
         def four(i, _):
@@ -169,9 +179,8 @@
             src_ref=src, dst_ref=dst, send_sem=send, recv_sem=recv, device_id=device, device_id_type=MESH
         )
 
-    def at_z(o):
-        return (2 * lax.rem(z + o, n_z) + core, c)
-
+    z_to = [lax.rem(z + o, n_z) for o in range(n_z)]
+    z_peers = [(2 * to + core, c) for to in z_to]
     near_first = sorted(range(1, n_z), key=lambda o: min(o, n_z - o))
     far_first = near_first[::-1]
     own_p = p_part(core, z)
@@ -197,19 +206,24 @@
         part = ref.at[k, phase, pl.ds(0, n_line - 1)]
         remote(part, part, line_send.at[k], sem.at[k, phase], sibling).wait_recv()
 
-    def send_squares(ref, ref_in, i, me, n, device):
+    def send_squares(ref, ref_in, w, me, n, device):
         ref_in[me] = ref[...]
-        for o in sorted(range(1, n), key=lambda o: -min(o, n - o)):
-            to = lax.rem(me + o, n)
-            remote(ref, ref_in.at[me], sq_send.at[i], sq_recv.at[i], device(to)).start()
+
+        def one(i, _):
+            to = lax.rem(me + n // 2 + i, n)
+            remote(ref, ref_in.at[me], sq_send.at[w], sq_recv.at[w], device(to)).start()
+            return 0
+
+        lax.fori_loop(0, n // 2, one, 0)
+        lax.fori_loop(n // 2 + 1, n, one, 0)
 
     def gradient_step(k):
-        for h in range(2):
-            pick_blocks(row_pick, dual[h * d_half:(h + 1) * d_half], h)
+        both = jnp.concatenate([dual[:d_half], dual[d_half:]], axis=1).astype(jnp.bfloat16)
+        picked[...] = jnp.dot(row_pick[...], both, preferred_element_type=jnp.float32).astype(jnp.bfloat16)
         grad[k, half_part(other)] = transposed_half(other)
         pair = {}
         for o in far_first + [0]:
-            to_z = lax.rem(z + o, n_z)
+            to_z = z_to[o]
             pair[o] = remote(
                 grad.at[k, p_part(other, to_z)], pair_in.at[k, z_part(to_z)],
                 pair_send.at[k], pair_recv.at[k, o], sibling,
@@ -217,11 +231,11 @@
             pair[o].start()
         grad[k, half_part(core)] = transposed_half(core)
         for o in far_first:
-            to_z = lax.rem(z + o, n_z)
+            to_z = z_to[o]
             pair[o].wait_recv()
             pair_sum[k, z_part(to_z)] = grad[k, p_part(core, to_z)] + pair_in[k, z_part(to_z)]
             remote(
-                pair_sum.at[k, z_part(to_z)], ring_in.at[k, o - 1], ring_send.at[k], ring_recv.at[k], at_z(o)
+                pair_sum.at[k, z_part(to_z)], ring_in.at[k, o - 1], ring_send.at[k], ring_recv.at[k], z_peers[o]
             ).start()
         pair[0].wait_recv()
         gradient = grad[k, own_p] + pair_in[k, z_part(z)]
@@ -232,10 +246,10 @@
         primal_new[k, own_p] = jnp.clip(primal[own_p] - tau * (cost[own_p] + gradient), 0.0, upper[own_p])
         mine = primal_new.at[k, own_p]
         for o in far_first:
-            remote(mine, mine, gather_send.at[k], gather_recv.at[k, o], at_z(o)).start()
+            remote(mine, mine, gather_send.at[k], gather_recv.at[k, o], z_peers[o]).start()
         remote(mine, mine, pass_send.at[k], pass_recv.at[k], sibling).start()
         for o in near_first:
-            here = primal_new.at[k, p_part(core, lax.rem(z + n_z - o, n_z))]
+            here = primal_new.at[k, p_part(core, z_to[n_z - o])]
             remote(here, here, gather_send.at[k], gather_recv.at[k, o], sibling).wait_recv()
             remote(here, here, pass_send.at[k], pass_recv.at[k], sibling).start()
 
@@ -290,6 +304,11 @@
         fresh = jnp.maximum(old + sigma * (loaded - capacity), 0.0)
         step = fresh - old
         dual_sq[pl.ds(k, 1), :] = jnp.sum(step * step, axis=0, keepdims=True)
+
+        @pl.when(k == ITERS - 1)
+        def _():
+            send_squares(dual_sq, dual_sq_in, 0, r, n_row, lambda to: (to, c))
+
         total = sum_dual[...] + fresh
         again = jnp.full((d_rows, LANES), flag) > 0.5
         dual[...] = jnp.where(again, total / jnp.full((d_rows, LANES), counter), fresh)
@@ -313,7 +332,6 @@
 
     lax.fori_loop(1, ITERS, iteration, counter)
 
-    send_squares(dual_sq, dual_sq_in, 0, r, n_row, lambda to: (to, c))
     weave(dual, dual_done)
     dual_copy = pltpu.make_async_copy(dual_done, dual_out, out_sem.at[1])
     dual_copy.start()
@@ -335,14 +353,15 @@
 
     sent(0, 0, True)
     lax.fori_loop(1, ITERS, sent, 0)
-    for i, (ref, n) in enumerate(((dual_sq_in, n_row), (primal_sq_in, n_col))):
+    def squares(ref, i, n):
         part = ref.at[pl.ds(0, n - 1)]
         whole = remote(part, part, sq_send.at[i], sq_recv.at[i], sibling)
         whole.wait_send()
         whole.wait_recv()
-    p_total = jnp.sum(jnp.sum(primal_sq_in[...], axis=0), axis=1, keepdims=True)
-    d_total = jnp.sum(jnp.sum(dual_sq_in[...], axis=0), axis=1, keepdims=True)
-    moves = jnp.sqrt(p_total / tau + d_total / sigma + 1e-6)
+        return jnp.sum(jnp.sum(ref[...], axis=0), axis=1, keepdims=True)
+
+    p_total = squares(primal_sq_in, 1, n_col) / tau
+    moves = jnp.sqrt(p_total + squares(dual_sq_in, 0, n_row) / sigma + 1e-6)
     move_out[...] = jnp.broadcast_to(moves, move_out.shape)
     pltpu.make_async_copy(primal_done, primal_out, out_sem.at[0]).wait()
     dual_copy.wait()

time: 101 us -> 99.7 us (0.987)
  Pallas kernels: 97.8 us -> 96.3 us
    pallas_call x1, Pallas kernels: 97.8 us -> 96.3 us  [shards(): pl.pallas_call(functools.partial(kernel, n_row, n_col), out_shape=out_sha...]
where the time goes in v4:
time: 99.7 us; the launch traced here: 99.6 us
  Pallas kernels  96.3 us (97%)
  local copies, waits for them, and re-layouts  1.98 us (2%)
  between operations  1.29 us (1%)
    pallas_call x1, Pallas kernels, shards(): pl.pallas_call(functools.partial(kernel, n_row, n_col), out_shape=out_sha...  96.3 us

profile of v4, /device:TPU:1, one launch (start us, length us, event | category | flops | bytes accessed | tf_op | source)
XLA Modules:
  0.0 99.6 jit_solution(4840066531321070267)
XLA Ops:
  1.3 96.3 %pdhg.1 = (f32[512,128]{1,0:T(8,128)S(1)}, f32[128,128]{1,0:T(8,128)S(1)}, f32[8,128]{1,0:T(8,128)S(1)}) custom-call(bf16[64,256,256]{2,1,0:T(8,128)(2,1)} %bitcast.10, s32[1,64]{1,0:T(1,128)} %bitcast.14, s32[1,64]{1,0:T(1,128)} %bitcast.15, f32[512,128]{1,0:T(8,128)} %bitcast.11, f32[512,128]{1,0:T(8,128)} %bitcast.12, f32[128,128]{1,0:T(8,128)} %bitcast.13, ...), custom_call_target="tpu_custom_call" | custom-call | tf_op jit(solution)/shard_map/pdhg/pallas_call | solution.py:384
  97.6 0.6 slice_reduce_fusion
  98.2 0.7 copy.15
  98.9 0.6 copy.16

commit v5 on v4

--- a/solution.py
+++ b/solution.py
@@ -9,7 +9,7 @@
 
 ITERS = 4
 LANES = 128
-GROUP = 16
+GROUP = 32
 VMEM_LIMIT = 48 * 2**20
 MESH = pl.DeviceIdType.MESH
 
@@ -266,8 +266,8 @@
 
     def load_step(k, counter, begin):
         x_in[k, 0, x] = jnp.dot(row_table[...], split(terms[:, :LANES]), preferred_element_type=jnp.float32)
+        y_in[k, 0, y] = jnp.dot(row_table[...], split(terms[:, LANES:]), preferred_element_type=jnp.float32)
         start_x(k, 0)
-        y_in[k, 0, y] = jnp.dot(row_table[...], split(terms[:, LANES:]), preferred_element_type=jnp.float32)
         start_y(k, 0)
 
         counter = counter + 1.0

time: 99.7 us -> 98.2 us (0.985)
  Pallas kernels: 96.3 us -> 94.8 us
    pallas_call x1, Pallas kernels: 96.3 us -> 94.8 us  [shards(): pl.pallas_call(functools.partial(kernel, n_row, n_col), out_shape=out_sha...]
where the time goes in v5:
time: 98.2 us; the launch traced here: 98.1 us
  Pallas kernels  94.8 us (97%)
  local copies, waits for them, and re-layouts  1.98 us (2%)
  between operations  1.29 us (1%)
    pallas_call x1, Pallas kernels, shards(): pl.pallas_call(functools.partial(kernel, n_row, n_col), out_shape=out_sha...  94.8 us

profile of v5, /device:TPU:1, one launch (start us, length us, event | category | flops | bytes accessed | tf_op | source)
XLA Modules:
  0.0 98.1 jit_solution(1064347510072259179)
XLA Ops:
  1.3 94.8 %pdhg.1 = (f32[512,128]{1,0:T(8,128)S(1)}, f32[128,128]{1,0:T(8,128)S(1)}, f32[8,128]{1,0:T(8,128)S(1)}) custom-call(bf16[64,256,256]{2,1,0:T(8,128)(2,1)} %bitcast.10, s32[1,64]{1,0:T(1,128)} %bitcast.14, s32[1,64]{1,0:T(1,128)} %bitcast.15, f32[512,128]{1,0:T(8,128)} %bitcast.11, f32[512,128]{1,0:T(8,128)} %bitcast.12, f32[128,128]{1,0:T(8,128)} %bitcast.13, ...), custom_call_target="tpu_custom_call" | custom-call | tf_op jit(solution)/shard_map/pdhg/pallas_call | solution.py:384
  96.1 0.6 slice_reduce_fusion
  96.7 0.7 copy.15
  97.5 0.6 copy.16
